TPU v7x, 512 devices: a whole 4x8x8 slice. The times are simulated.
512 devices in a mesh: group: 32 (over z, x), tensor: 16 (over y, core).
Axes of the slice: x: 4, y: 8, z: 8, core: 2. Of those that a mesh axis runs over, the one named last changes fastest.
Arguments:
- tokens: bfloat16 [16384, 8192], P('group', 'tensor'), may hold values from -6 to 6
- token_slot_index: int32 [16384], P('group'), may hold values from 0 to 15
- group_slot_adapters: int32 [32, 16], replicated, may hold values from 0 to 511, as said below
- adapter_storage_position: int32 [512], replicated, may hold values from 0 to 511, as said below
- query_weight: bfloat16 [8192, 4096], P(None, 'tensor'), may hold values from -0.0625 to 0.0625
- down_weight: bfloat16 [512, 16, 8192], P(('group', 'tensor')), may hold values from -0.0625 to 0.0625
- up_weight: bfloat16 [512, 16, 4096], P(('group', 'tensor')), may hold values from -1.5 to 1.5
Outputs:
- queries: bfloat16 [16384, 4096], P('group', 'tensor')
Inputs may be any that keep to these rules, and one draw needn't show every extreme that they name: `group_slot_adapters`: each row names 16 different adapters. Positions are grouped in blocks of 16 consecutive ones; at most 1 adapters of one row have positions in one block, and in every row some block holds exactly 1. `adapter_storage_position`: A permutation.
All inputs are finite; a program needn't handle non-finite values.
Results may differ from a plain program's by a relative error of at most 0.0029.
Values may be sent and summed in bfloat16 or wider, within the bound.
A program may use at most 64 MiB of HBM per device.

v0:
```python
import jax
import jax.numpy as jnp
from jax import lax
from jax.sharding import PartitionSpec as P

ADAPTER_RANK = 16
GROUP_SLOTS = 16


ADAPTER_SCALE = 0.5


def body(
    tokens,
    token_slot_index,
    group_slot_adapters,
    adapter_storage_position,
    query_weight,
    down_weight,
    up_weight,
):
    tensor_shard_count = lax.axis_size("tensor")
    group_count = lax.axis_size("group")
    group_index = lax.axis_index("group")
    per_owner = (GROUP_SLOTS + group_count - 1) // group_count
    resident_count = tensor_shard_count * down_weight.shape[0]
    down_panel, up_panel = (
        lax.all_to_all(down_weight, "tensor", split_axis=2, concat_axis=0, tiled=True),
        lax.all_to_all(up_weight, "tensor", split_axis=2, concat_axis=0, tiled=True),
    )
    store_size = adapter_storage_position.shape[0]
    matches = (
        group_slot_adapters[:, :, None] == jnp.arange(store_size, dtype=jnp.int32)[None, None, :]
    )
    storage_places = jnp.sum(jnp.where(matches, adapter_storage_position[None, None, :], 0), axis=2)
    owner_group = storage_places // resident_count
    local_index = storage_places % resident_count
    slot_grid = jnp.arange(GROUP_SLOTS, dtype=jnp.int32)
    same_owner = owner_group[:, :, None] == owner_group[:, None, :]
    before = slot_grid[None, :] < slot_grid[:, None]
    order_rank = jnp.sum((same_owner & before[None, :, :]).astype(jnp.int32), axis=2)
    owned_here = owner_group == group_index
    cap_grid = jnp.arange(per_owner, dtype=jnp.int32)
    local_grid = jnp.arange(resident_count, dtype=jnp.int32)
    select = (
        owned_here[:, :, None, None]
        & (order_rank[:, :, None, None] == cap_grid[None, None, :, None])
        & (local_index[:, :, None, None] == local_grid[None, None, None, :])
    )
    select = jnp.sum(select.astype(jnp.float32), axis=1).astype(jnp.bfloat16)
    send_a = jnp.einsum(
        "gcl,lrd->gcrd", select, down_panel, preferred_element_type=jnp.float32
    ).astype(jnp.bfloat16)
    send_b = jnp.einsum(
        "gcl,lrd->gcrd", select, up_panel, preferred_element_type=jnp.float32
    ).astype(jnp.bfloat16)
    recv_a, recv_b = (
        lax.all_to_all(send_a, "group", split_axis=0, concat_axis=0, tiled=True),
        lax.all_to_all(send_b, "group", split_axis=0, concat_axis=0, tiled=True),
    )
    row_owner = lax.dynamic_index_in_dim(owner_group, group_index, 0, keepdims=False)
    row_rank = lax.dynamic_index_in_dim(order_rank, group_index, 0, keepdims=False)
    flat_grid = jnp.arange(group_count * per_owner, dtype=jnp.int32)
    slot_pick = ((row_owner * per_owner + row_rank)[:, None] == flat_grid[None, :]).astype(
        jnp.bfloat16
    )
    width_a = down_panel.shape[2]
    width_b = up_panel.shape[2]
    slot_a = jnp.dot(
        slot_pick,
        recv_a.reshape(group_count * per_owner, ADAPTER_RANK * width_a),
        preferred_element_type=jnp.float32,
    )
    slot_a = slot_a.astype(jnp.bfloat16).reshape(GROUP_SLOTS * ADAPTER_RANK, width_a)
    slot_b = jnp.dot(
        slot_pick,
        recv_b.reshape(group_count * per_owner, ADAPTER_RANK * width_b),
        preferred_element_type=jnp.float32,
    )
    slot_b = slot_b.astype(jnp.bfloat16).reshape(GROUP_SLOTS * ADAPTER_RANK, width_b)
    choose = token_slot_index[:, None] == slot_grid[None, :]
    choose_float = choose.astype(jnp.float32)
    row_count = tokens.shape[0]
    all_slots = lax.dot_general(
        tokens, slot_a, (((1,), (1,)), ((), ())), preferred_element_type=jnp.float32
    )
    partial_value = jnp.sum(
        all_slots.reshape(row_count, GROUP_SLOTS, ADAPTER_RANK) * choose_float[:, :, None], axis=1
    )
    shrink = lax.psum(partial_value, "tensor")
    base_contribution = jnp.dot(
        lax.all_gather(tokens, "tensor", axis=1, tiled=True),
        query_weight,
        preferred_element_type=jnp.float32,
    )
    low_rank = shrink.astype(jnp.bfloat16)
    spread_rows = (choose.astype(jnp.bfloat16)[:, :, None] * low_rank[:, None, :]).reshape(
        row_count, GROUP_SLOTS * ADAPTER_RANK
    )
    adapter_contribution = jnp.dot(spread_rows, slot_b, preferred_element_type=jnp.float32)
    return (base_contribution + ADAPTER_SCALE * adapter_contribution).astype(jnp.bfloat16)


def solution(mesh):
    in_specs = (
        P("group", "tensor"),
        P("group"),
        P(),
        P(),
        P(None, "tensor"),
        P(("group", "tensor"), None, None),
        P(("group", "tensor"), None, None),
    )
    out_specs = P("group", "tensor")
    return jax.shard_map(body, mesh=mesh, in_specs=in_specs, out_specs=out_specs, check_vma=False)
```

profile of v0, /device:TPU:1, one launch (start us, length us, event | category | flops | bytes accessed | tf_op | source)
XLA Modules:
  0.0 235.5 jit_solution(5915801782960044394)
XLA Ops:
  6.5 0.7 all-gather.2.cloned.1.call-update
  7.3 4.3 %copy.52 = bf16[1,16,4096]{1,0,2:T(2,128)(2,1)S(1)} copy(bf16[1,16,4096]{2,1,0:T(8,128)(2,1)} %param.13) | data formatting | bytes 262144 | tf_op args[6]
  11.6 0.5 broadcast.185
  12.1 22.4 %reduce.4 = bf16[4096,16]{1,0:T(8,128)(2,1)S(1)} reduce(bf16[4096,1,16]{2,1,0:T(2,128)(2,1)S(1)} %bitcast.59, bf16[]{:T(256)} %broadcast.185), dimensions={1}, to_apply=%bitcast.43.reduce_sub_computation | reduce | bytes 262146
  34.5 1.8 reshape.208
  36.3 10.2 %all-to-all-start.2 = ((bf16[16,2,2048]{2,1,0:T(2,128)(2,1)}), bf16[16,2,2048]{2,1,0:T(2,128)(2,1)S(1)}, u32[]{:S(2)}, u32[]{:S(2)}) async-start(bf16[16,2,2048]{2,1,0:T(2,128)(2,1)} %reshape.208), calls=%async_computation.2 | async-start | bytes 262144 | tf_op jit(solution)/shard_map/all_to_all | solution.py:29
  46.5 0.7 select_reduce_fusion
  47.3 6.7 %copy.49 = bf16[1,16,8192]{1,0,2:T(2,128)(2,1)} copy(bf16[1,16,8192]{2,1,0:T(8,128)(2,1)S(1)} %copy-done.1) | data formatting | bytes 524288 | tf_op args[5]
  54.1 45.2 %reduce.3 = bf16[8192,16]{1,0:T(8,128)(2,1)S(1)} reduce(bf16[8192,1,16]{2,1,0:T(2,128)(2,1)} %bitcast.57, bf16[]{:T(256)} %broadcast.185), dimensions={1}, to_apply=%bitcast.41.reduce_sub_computation | reduce | bytes 524290
  99.3 2.8 %reshape.206 = bf16[16,2,4096]{2,1,0:T(2,128)(2,1)} reshape(bf16[8192,16]{1,0:T(8,128)(2,1)S(1)} %reduce.3) | data formatting | bytes 524288
  102.2 7.3 %all-to-all-start = ((bf16[16,2,4096]{2,1,0:T(2,128)(2,1)}), bf16[16,2,4096]{2,1,0:T(2,128)(2,1)S(1)}, u32[]{:S(2)}, u32[]{:S(2)}) async-start(bf16[16,2,4096]{2,1,0:T(2,128)(2,1)} %reshape.206), calls=%async_computation | async-start | bytes 524288 | tf_op jit(solution)/shard_map/all_to_all | solution.py:28
  109.6 1.8 reshape.209
  111.5 2.0 copy.53
  113.5 0.2 fusion.3
  113.7 0.9 copy.54
  114.6 6.6 %all-to-all-done = bf16[16,2,4096]{2,1,0:T(2,128)(2,1)S(1)} async-done(((bf16[16,2,4096]{2,1,0:T(2,128)(2,1)}), bf16[16,2,4096]{2,1,0:T(2,128)(2,1)S(1)}, u32[]{:S(2)}, u32[]{:S(2)}) %all-to-all-start) | async-done | bytes 262176 | tf_op jit(solution)/shard_map/all_to_all | solution.py:28
  121.2 11.3 %all-to-all-start.3 = ((bf16[32,1,16,256]{3,2,1,0:T(8,128)(2,1)}), bf16[32,1,16,256]{3,2,1,0:T(8,128)(2,1)S(1)}, u32[]{:S(2)}, u32[]{:S(2)}) async-start(bf16[32,1,16,256]{3,2,1,0:T(8,128)(2,1)} %copy.54), calls=%async_computation.3 | async-start | bytes 524288 | tf_op jit(solution)/shard_map/all_to_all | solution.py:59
  132.4 7.7 %reshape.207 = bf16[8192,1,16]{2,1,0:T(2,128)(2,1)} reshape(bf16[16,2,4096]{2,1,0:T(2,128)(2,1)S(1)} %all-to-all-done) | data formatting | bytes 524288
  140.1 7.9 %copy.50 = bf16[1,16,8192]{2,1,0:T(8,128)(2,1)S(1)} copy(bf16[1,16,8192]{1,0,2:T(2,128)(2,1)} %bitcast.58) | data formatting | bytes 524288 | tf_op jit(solution)/shard_map/all_to_all | solution.py:28
  148.1 0.3 fusion
  148.4 1.1 copy.51
  149.6 9.2 %all-to-all-start.1 = ((bf16[32,1,16,512]{3,2,1,0:T(8,128)(2,1)}), bf16[32,1,16,512]{3,2,1,0:T(8,128)(2,1)S(1)}, u32[]{:S(2)}, u32[]{:S(2)}) async-start(bf16[32,1,16,512]{3,2,1,0:T(8,128)(2,1)} %copy.51), calls=%async_computation.1 | async-start | bytes 1048576 | tf_op jit(solution)/shard_map/all_to_all | solution.py:58
  158.8 0.2 add_reduce_fusion
  159.1 0.2 convolution_convert_fusion.1
  159.4 16.1 %all-to-all-done.1 = bf16[32,1,16,512]{3,2,1,0:T(8,128)(2,1)S(1)} async-done(((bf16[32,1,16,512]{3,2,1,0:T(8,128)(2,1)}), bf16[32,1,16,512]{3,2,1,0:T(8,128)(2,1)S(1)}, u32[]{:S(2)}, u32[]{:S(2)}) %all-to-all-start.1) | async-done | bytes 524320 | tf_op jit(solution)/shard_map/all_to_all | solution.py:58
  175.5 0.3 copy.56
  175.8 0.3 convolution_convert_fusion
  176.1 0.1 reshape.200
  176.2 0.3 fusion.16
  176.6 44.1 %psum.7 = bf16[512,16]{0,1:T(8,128)(2,1)S(1)} all-reduce(f32[512,16]{0,1:T(8,128)S(1)} %multiply_reduce_fusion), channel_id=1, replica_groups=mesh['group'=32,'tensor'=16] {'tensor'}, use_global_device_ids=true, to_apply=%region_4.5 | all-reduce | flops 8192 | bytes 49152 | tf_op jit(solution)/shard_map/psum | solution.py:90
  220.8 6.9 %fusion.15 = f32[512,256]{1,0:T(8,128)S(1)} fusion(bf16[512,8192]{1,0:T(8,128)(2,1)} %all-gather.2.cloned.1.call-done, bf16[8192,256]{1,0:T(8,128)(2,1)} %param.11), kind=kOutput, calls=%fused_computation.40 | convolution fusion | flops 2147483648 | bytes 13107200 | tf_op jit(solution)/shard_map/dot_general | solution.py:91
  227.7 1.0 fusion.2
  (28 shorter events, 0.7 us)
Async XLA Ops:
  6.5 39.9 %copy-start.2 = (s32[32,16]{0,1:T(8,128)S(1)}, s32[32,16]{0,1:T(8,128)}, u32[]{:S(2)}) copy-start(s32[32,16]{0,1:T(8,128)} %param.9) | copy-start | bytes 6148
  6.5 40.0 %copy-start.3 = (s32[512]{0:T(512)S(1)}, s32[512]{0:T(512)}, u32[]{:S(2)}) copy-start(s32[512]{0:T(512)} %param.10) | copy-start | bytes 6148
  6.5 40.8 %copy-start.1 = (bf16[1,16,8192]{2,1,0:T(8,128)(2,1)S(1)}, bf16[1,16,8192]{2,1,0:T(8,128)(2,1)}, u32[]{:S(2)}) copy-start(bf16[1,16,8192]{2,1,0:T(8,128)(2,1)} %param.12) | copy-start | bytes 786436
  6.5 214.2 %all-gather.2.cloned.1.call-start = ((), (), s32[]{:S(2)}) async-start(), calls=%async_computation.4 | async-start | bytes 8912896 | tf_op jit(solution)/shard_map/all_gather | solution.py:92
  36.3 65.9 %all-to-all-start.2 = ((bf16[16,2,2048]{2,1,0:T(2,128)(2,1)}), bf16[16,2,2048]{2,1,0:T(2,128)(2,1)S(1)}, u32[]{:S(2)}, u32[]{:S(2)}) async-start(bf16[16,2,2048]{2,1,0:T(2,128)(2,1)} %reshape.208), calls=%async_computation.2 | async-start | bytes 262144 | tf_op jit(solution)/shard_map/all_to_all | solution.py:29
  102.2 19.0 %all-to-all-start = ((bf16[16,2,4096]{2,1,0:T(2,128)(2,1)}), bf16[16,2,4096]{2,1,0:T(2,128)(2,1)S(1)}, u32[]{:S(2)}, u32[]{:S(2)}) async-start(bf16[16,2,4096]{2,1,0:T(2,128)(2,1)} %reshape.206), calls=%async_computation | async-start | bytes 524288 | tf_op jit(solution)/shard_map/all_to_all | solution.py:28
  121.2 28.4 %all-to-all-start.3 = ((bf16[32,1,16,256]{3,2,1,0:T(8,128)(2,1)}), bf16[32,1,16,256]{3,2,1,0:T(8,128)(2,1)S(1)}, u32[]{:S(2)}, u32[]{:S(2)}) async-start(bf16[32,1,16,256]{3,2,1,0:T(8,128)(2,1)} %copy.54), calls=%async_computation.3 | async-start | bytes 524288 | tf_op jit(solution)/shard_map/all_to_all | solution.py:59
  140.1 18.9 %copy-start.4 = (s32[512]{0:T(512)S(1)}, s32[512]{0:T(512)}, u32[]{:S(2)}) copy-start(s32[512]{0:T(512)} %param.8) | copy-start | bytes 6148
  148.0 28.2 %copy-start = (bf16[512,512]{1,0:T(8,128)(2,1)S(1)}, bf16[512,512]{1,0:T(8,128)(2,1)}, u32[]{:S(2)}) copy-start(bf16[512,512]{1,0:T(8,128)(2,1)} %param.7) | copy-start | bytes 1572868
  149.6 25.9 %all-to-all-start.1 = ((bf16[32,1,16,512]{3,2,1,0:T(8,128)(2,1)}), bf16[32,1,16,512]{3,2,1,0:T(8,128)(2,1)S(1)}, u32[]{:S(2)}, u32[]{:S(2)}) async-start(bf16[32,1,16,512]{3,2,1,0:T(8,128)(2,1)} %copy.51), calls=%async_computation.1 | async-start | bytes 1048576 | tf_op jit(solution)/shard_map/all_to_all | solution.py:58
Sparse Core Ops, SparseCore 0:
  9.5 66.9 all-gather.1
where the time goes:
time: 238 us; the launch traced here: 236 us
  other arithmetic  68.8 us (29%)
  blocking collectives  44.1 us (19%)
  local copies, waits for them, and re-layouts  38.3 us (16%)
  starting transfers between devices  38 us (16%)
  waiting for transfers between devices  23.4 us (10%)
  between operations  13.6 us (6%)
  matrix products  9.27 us (4%)
    unnamed x2, other arithmetic  67.6 us
    psum x1, blocking collectives, body(): shrink = lax.psum(partial_value, 'tensor')  44.1 us
    unnamed x22, local copies, waits for them, and re-layouts  26.2 us
    all_to_all x1, waiting for transfers between devices, body(): lax.all_to_all(send_a, 'group', split_axis=0, concat_axis=0, tiled=True)  16.1 us
    all_to_all x1, starting transfers between devices, body(): lax.all_to_all(send_b, 'group', split_axis=0, concat_axis=0, tiled=True)  11.3 us
    all_to_all x1, starting transfers between devices, body(): lax.all_to_all(up_weight, 'tensor', split_axis=2, concat_axis=0, tiled=True)  10.2 us
    all_to_all x1, starting transfers between devices, body(): lax.all_to_all(send_a, 'group', split_axis=0, concat_axis=0, tiled=True)  9.21 us
    all_to_all x1, local copies, waits for them, and re-layouts, body(): lax.all_to_all(down_weight, 'tensor', split_axis=2, concat_axis=0, tiled=...  7.87 us
  transfers between devices with their start and end apart: 5, of which 2 were waited for; matrix products, arithmetic and copies ran while one was open for 46% of the time, Pallas kernels for 0%

commit v1 on v0

v1 whole, which is shorter than its diff:
```python
import functools

import jax
import jax.numpy as jnp
from jax import lax
from jax.experimental import pallas as pl
from jax.experimental.pallas import tpu as pltpu
from jax.sharding import PartitionSpec as P

RANK = 16
SLOTS = 16
SCALE = 0.5
NZ, NX, NY, NC = 8, 4, 8, 2
NG, NT = NZ * NX, NY * NC
ROWS = 512
KB = 512
NB = 256
CH = 4
CR = ROWS // CH
MESH = pl.DeviceIdType.MESH


def kernel(
    gsa, asp, idx_ref, tok, w_hbm, down, up, out_ref,
    xall, w_v, panel, staged, inbox, slots, acc, part, rs, lr, lr2, local_of,
    w_sem, x_sem, own_sem,
    ya_send, ya_recv, ga_send, ga_recv,
    ring_send, ring_recv, cross_send, cross_recv,
    rs_send, rs_recv, lr_send, lr_recv,
):
    g = lax.axis_index("group")
    t = lax.axis_index("tensor")
    y = t // NC
    c = t % NC
    other = y * NC + (1 - c)

    def tensor_peer(i):
        return lax.rem(t + i, NT)

    def group_peer(j):
        return lax.rem(g + j, NG)

    barrier = pltpu.get_barrier_semaphore()

    @pl.loop(1, NT)
    def _(i):
        pl.semaphore_signal(barrier, inc=1, device_id={"group": g, "tensor": tensor_peer(i)}, device_id_type=MESH)

    @pl.loop(1, NG)
    def _(j):
        pl.semaphore_signal(barrier, inc=1, device_id={"group": group_peer(j), "tensor": t}, device_id_type=MESH)

    w_copy = pltpu.make_async_copy(w_hbm, w_v, w_sem)
    x_copy = pltpu.make_async_copy(tok, xall.at[t], x_sem)
    down_own = pltpu.make_async_copy(
        down.at[0, :, pl.ds(pl.multiple_of(t * KB, KB), KB)], panel.at[t, :, 0:KB], own_sem.at[0])
    up_own = pltpu.make_async_copy(
        up.at[0, :, pl.ds(pl.multiple_of(t * NB, NB), NB)], panel.at[t, :, KB:KB + NB], own_sem.at[1])
    down_own.start()
    up_own.start()
    x_copy.start()
    w_copy.start()

    pl.semaphore_wait(barrier, NT - 1 + NG - 1)

    def ya_copies(i):
        dst = tensor_peer(i)
        dev = {"group": g, "tensor": dst}
        return (
            pltpu.make_async_remote_copy(
                down.at[0, :, pl.ds(pl.multiple_of(dst * KB, KB), KB)], panel.at[t, :, 0:KB],
                ya_send.at[i], ya_recv.at[i], device_id=dev, device_id_type=MESH),
            pltpu.make_async_remote_copy(
                up.at[0, :, pl.ds(pl.multiple_of(dst * NB, NB), NB)], panel.at[t, :, KB:KB + NB],
                ya_send.at[i], ya_recv.at[i], device_id=dev, device_id_type=MESH),
        )

    @pl.loop(1, NT)
    def _(i):
        a, b = ya_copies(i)
        a.start()
        b.start()

    def ring_copy(src, block, d, k, way):
        dst_y = lax.rem(y + (1 if way == 0 else NY - 1), NY)
        rows = slice(k * CR, (k + 1) * CR)
        return pltpu.make_async_remote_copy(
            src.at[rows, :], xall.at[block, rows, :],
            ring_send.at[way, d - 1, k], ring_recv.at[way, d - 1, k],
            device_id={"group": g, "tensor": dst_y * NC + c}, device_id_type=MESH)

    def cross_copy(src, block, h, k):
        rows = slice(k * CR, (k + 1) * CR)
        return pltpu.make_async_remote_copy(
            src.at[rows, :], xall.at[block, rows, :],
            cross_send.at[h, k], cross_recv.at[h, k],
            device_id={"group": g, "tensor": other}, device_id_type=MESH)

    def reaches(way, d, k):
        if d < NY // 2:
            return True
        return d == NY // 2 and (k < CH // 2) == (way == 0)

    def source(way, d):
        ys = lax.rem(y + (NY - d if way == 0 else d), NY)
        return ys * NC + c, ys * NC + (1 - c)

    for k in range(CH):
        for way in (0, 1):
            ring_copy(tok, t, 1, k, way).start()
        cross_copy(tok, t, 0, k).start()

    @pl.loop(0, NG)
    def _(r):
        pick = jnp.int32(0)
        for s in range(SLOTS):
            place = asp[gsa[r, s]]
            pick = pick + jnp.where(lax.shift_right_logical(place, 4) == g, place & 15, 0)
        local_of[r] = pick

    down_own.wait()
    up_own.wait()

    @pl.loop(1, NT)
    def _(i):
        block = panel.at[lax.rem(t + NT - i, NT)]
        pltpu.make_async_remote_copy(
            block, block, ya_send.at[i], ya_recv.at[i],
            device_id={"group": g, "tensor": tensor_peer(i)}, device_id_type=MESH).wait_recv()

    def ga_copy(j):
        dst = group_peer(j)
        return pltpu.make_async_remote_copy(
            staged.at[j], inbox.at[g], ga_send.at[j], ga_recv.at[j],
            device_id={"group": dst, "tensor": t}, device_id_type=MESH)

    @pl.loop(1, NG)
    def _(j):
        staged[j] = panel[local_of[group_peer(j)]]
        ga_copy(j).start()

    inbox[g] = panel[local_of[g]]

    x_copy.wait()
    w_copy.wait()

    def weight(block):
        return w_v[pl.ds(pl.multiple_of(block * KB, KB), KB), :]

    acc[...] = jnp.dot(xall[t], weight(t), preferred_element_type=jnp.float32)

    def accumulate(block):
        acc[...] += jnp.dot(xall[block], weight(block), preferred_element_type=jnp.float32)

    def cross_wait(h, block):
        for k in range(CH):
            cross_copy(xall.at[block], block, h, k).wait_recv()

    def ring_step(d):
        for k in range(CH):
            for way in (0, 1):
                if not reaches(way, d, k):
                    continue
                block, _ = source(way, d)
                ring_copy(xall.at[block], block, d, k, way).wait_recv()
                if reaches(way, d + 1, k):
                    ring_copy(xall.at[block], block, d + 1, k, way).start()
                h = d if way == 0 or d == NY // 2 else NY - d
                cross_copy(xall.at[block], block, h, k).start()

    def blocks_at(d):
        return (0,) if d == NY // 2 else (0, 1)

    def ring_own(d):
        for way in blocks_at(d):
            accumulate(source(way, d)[0])

    def ring_cross(d):
        for way in blocks_at(d):
            h = d if way == 0 else NY - d
            block = source(way, d)[1]
            cross_wait(h, block)
            accumulate(block)

    ring_step(1)
    ring_own(1)
    cross_wait(0, other)
    accumulate(other)
    ring_step(2)
    ring_own(2)
    ring_cross(1)

    @pl.loop(1, NG)
    def _(j):
        src = lax.rem(g + NG - j, NG)
        pltpu.make_async_remote_copy(
            inbox.at[src], inbox.at[src], ga_send.at[j], ga_recv.at[j],
            device_id={"group": group_peer(j), "tensor": t}, device_id_type=MESH).wait_recv()

    for s in range(SLOTS):
        owner = lax.shift_right_logical(asp[gsa[g, s]], 4)
        slots[s * RANK:(s + 1) * RANK, :] = inbox[owner]

    idx = idx_ref[...]
    every = lax.dot_general(
        slots[:, 0:KB], xall[t], (((1,), (1,)), ((), ())), preferred_element_type=jnp.float32)
    partial = jnp.zeros((RANK, ROWS), jnp.float32)
    for s in range(SLOTS):
        partial = partial + jnp.where(idx == s, every[s * RANK:(s + 1) * RANK, :], 0.0)
    for r in range(RANK):
        part[r] = partial[r:r + 1, :]

    def rs_copy(i):
        dst = tensor_peer(i)
        return pltpu.make_async_remote_copy(
            part.at[dst], rs.at[t], rs_send.at[i], rs_recv.at[i],
            device_id={"group": g, "tensor": dst}, device_id_type=MESH)

    @pl.loop(1, NT)
    def _(i):
        rs_copy(i).start()

    rs[t] = part[t]

    ring_step(3)
    ring_own(3)

    @pl.loop(1, NT)
    def _(i):
        src = lax.rem(t + NT - i, NT)
        pltpu.make_async_remote_copy(
            rs.at[src], rs.at[src], rs_send.at[i], rs_recv.at[i],
            device_id={"group": g, "tensor": tensor_peer(i)}, device_id_type=MESH).wait_recv()

    total = rs[0]
    for i in range(1, NT):
        total = total + rs[i]
    lr[t] = total

    def lr_copy(i):
        return pltpu.make_async_remote_copy(
            lr.at[t], lr.at[t], lr_send.at[i], lr_recv.at[i],
            device_id={"group": g, "tensor": tensor_peer(i)}, device_id_type=MESH)

    @pl.loop(1, NT)
    def _(i):
        lr_copy(i).start()

    ring_cross(2)

    @pl.loop(1, NT)
    def _(i):
        block = panel.at[t]
        pltpu.make_async_remote_copy(
            block, block, ya_send.at[i], ya_recv.at[i],
            device_id={"group": g, "tensor": tensor_peer(i)}, device_id_type=MESH).wait_send()

    @pl.loop(1, NG)
    def _(j):
        ga_copy(j).wait_send()

    @pl.loop(1, NT)
    def _(i):
        rs_copy(i).wait_send()

    @pl.loop(1, NT)
    def _(i):
        src = lax.rem(t + NT - i, NT)
        pltpu.make_async_remote_copy(
            lr.at[src], lr.at[src], lr_send.at[i], lr_recv.at[i],
            device_id={"group": g, "tensor": tensor_peer(i)}, device_id_type=MESH).wait_recv()

    for r in range(RANK):
        lr2[r:r + 1, :] = lr[r]
    low = lr2[...].astype(jnp.bfloat16).astype(jnp.float32)
    spread = jnp.concatenate([jnp.where(idx == s, low, 0.0) for s in range(SLOTS)], axis=0)
    spread = jnp.transpose(spread).astype(jnp.bfloat16)
    adapter = jnp.dot(spread, slots[:, KB:KB + NB], preferred_element_type=jnp.float32)
    acc[...] += SCALE * adapter

    ring_cross(3)
    ring_step(4)
    ring_own(4)

    @pl.loop(1, NT)
    def _(i):
        lr_copy(i).wait_send()

    for k in range(CH):
        for way in (0, 1):
            for d in range(1, NY // 2 + 1):
                if reaches(way, d, k):
                    ring_copy(xall.at[t], t, d, k, way).wait_send()

    h = NY // 2
    block = source(0, h)[1]
    cross_wait(h, block)
    out_ref[...] = (acc[...] + jnp.dot(
        xall[block], weight(block), preferred_element_type=jnp.float32)).astype(out_ref.dtype)
    for k in range(CH):
        for h in range(NY):
            cross_copy(xall.at[t], t, h, k).wait_send()


def body(tokens, token_slot_index, group_slot_adapters, adapter_storage_position, query_weight, down_weight, up_weight):
    any_space = pl.BlockSpec(memory_space=pl.ANY)
    vmem = pl.BlockSpec(memory_space=pltpu.VMEM)
    smem = pl.BlockSpec(memory_space=pltpu.SMEM)
    dma = pltpu.SemaphoreType.DMA
    bf16, f32 = jnp.bfloat16, jnp.float32
    return pl.pallas_call(
        kernel,
        out_shape=jax.ShapeDtypeStruct((ROWS, NB), bf16),
        in_specs=[smem, smem, vmem, any_space, any_space, any_space, any_space],
        out_specs=vmem,
        scratch_shapes=[
            pltpu.VMEM((NT, ROWS, KB), bf16),
            pltpu.VMEM((NT * KB, NB), bf16),
            pltpu.VMEM((NT, RANK, KB + NB), bf16),
            pltpu.VMEM((NG, RANK, KB + NB), bf16),
            pltpu.VMEM((NG, RANK, KB + NB), bf16),
            pltpu.VMEM((SLOTS * RANK, KB + NB), bf16),
            pltpu.VMEM((ROWS, NB), f32),
            pltpu.VMEM((RANK, 1, ROWS), f32),
            pltpu.VMEM((NT, 1, ROWS), f32),
            pltpu.VMEM((NT, 1, ROWS), f32),
            pltpu.VMEM((RANK, ROWS), f32),
            pltpu.SMEM((NG,), jnp.int32),
            dma, dma, dma((2,)),
            dma((NT,)), dma((NT,)), dma((NG,)), dma((NG,)),
            dma((2, NY // 2, CH)), dma((2, NY // 2, CH)), dma((NY, CH)), dma((NY, CH)),
            dma((NT,)), dma((NT,)), dma((NT,)), dma((NT,)),
        ],
        compiler_params=pltpu.CompilerParams(
            collective_id=0, has_side_effects=True, vmem_limit_bytes=48 * 1024 * 1024),
        cost_estimate=pl.CostEstimate(flops=2 * ROWS * NT * KB * NB, bytes_accessed=8 << 20, transcendentals=0),
    )(group_slot_adapters, adapter_storage_position, token_slot_index.reshape(1, ROWS),
      tokens, query_weight, down_weight, up_weight)


def solution(mesh):
    in_specs = (
        P("group", "tensor"),
        P("group"),
        P(),
        P(),
        P(None, "tensor"),
        P(("group", "tensor"), None, None),
        P(("group", "tensor"), None, None),
    )
    return jax.shard_map(body, mesh=mesh, in_specs=in_specs, out_specs=P("group", "tensor"), check_vma=False)
```

time: 238 us -> 84 us (0.35)
  Pallas kernels: 0 us -> 75.7 us
  other arithmetic: 68.8 us -> 0 us
  blocking collectives: 44.1 us -> 0 us
  starting transfers between devices: 38 us -> 0 us
  local copies, waits for them, and re-layouts: 38.3 us -> 7.92 us
  waiting for transfers between devices: 23.4 us -> 0 us
  between operations: 13.6 us -> 0.02 us
  matrix products: 9.27 us -> 0 us
    pallas_call x0 -> x1, Pallas kernels: none -> 75.7 us  [body(): pl.pallas_call(kernel, out_shape=jax.ShapeDtypeStruct((ROWS, NB), bf16),...]
    unnamed x2 -> x0, other arithmetic: 67.6 us -> none
    psum x1 -> x0, blocking collectives: 44.1 us -> none  [body(): shrink = lax.psum(partial_value, 'tensor')]
    all_to_all x4 -> x0, starting transfers between devices: 37.9 us -> none  [the longest x1 11.3 us: body(): lax.all_to_all(send_b, 'group', split_axis=0, concat_axis=0, tiled=True)]
    all_to_all x4 -> x0, waiting for transfers between devices: 22.7 us -> none  [the longest x1 16.1 us: body(): lax.all_to_all(send_a, 'group', split_axis=0, concat_axis=0, tiled=True)]
    unnamed x22 -> x14, local copies, waits for them, and re-layouts: 26.2 us -> 7.92 us
    all_to_all x2 -> x0, local copies, waits for them, and re-layouts: 9.86 us -> none  [the longest x1 7.87 us: body(): lax.all_to_all(down_weight, 'tensor', split_axis=2, concat_axis=0, tiled=...]
    dot_general x7 -> x0, matrix products: 9.27 us -> none  [the longest x1 6.9 us: body(): jnp.dot(lax.all_gather(tokens, 'tensor', axis=1, tiled=True), query_weigh...]
  transfers between devices with their start and end apart: 5 -> 0, of which waited for: 2 -> 0; matrix products, arithmetic and copies ran while one was open for 46% -> 0% of each run, Pallas kernels for 0% -> 0%
where the time goes in v1:
time: 84 us; the launch traced here: 83.6 us
  Pallas kernels  75.7 us (90%)
  local copies, waits for them, and re-layouts  7.92 us (9%)
    pallas_call x1, Pallas kernels, body(): pl.pallas_call(kernel, out_shape=jax.ShapeDtypeStruct((ROWS, NB), bf16),...  75.7 us
    unnamed x14, local copies, waits for them, and re-layouts  7.92 us

profile of v1, /device:TPU:1, one launch (start us, length us, event | category | flops | bytes accessed | tf_op | source)
XLA Modules:
  0.0 83.6 jit_solution(15156419685098257900)
XLA Ops:
  0.0 0.8 copy.8.gsa
  0.8 0.0 copy-start
  0.8 2.2 %copy-done = bf16[8192,256]{1,0:T(8,128)(2,1)S(1)} copy-done((bf16[8192,256]{1,0:T(8,128)(2,1)S(1)}, bf16[8192,256]{1,0:T(8,128)(2,1)}, u32[]{:S(2)}) %copy-start) | copy-done | bytes 4194328
  3.0 0.0 copy-start.1
  3.0 1.0 %copy-done.1 = bf16[512,512]{1,0:T(8,128)(2,1)S(1)} copy-done((bf16[512,512]{1,0:T(8,128)(2,1)S(1)}, bf16[512,512]{1,0:T(8,128)(2,1)}, u32[]{:S(2)}) %copy-start.1) | copy-done | bytes 524312
  4.0 0.0 copy-start.2
  4.0 0.9 %copy-done.2 = bf16[1,16,8192]{2,1,0:T(8,128)(2,1)S(1)} copy-done((bf16[1,16,8192]{2,1,0:T(8,128)(2,1)S(1)}, bf16[1,16,8192]{2,1,0:T(8,128)(2,1)}, u32[]{:S(2)}) %copy-start.2) | copy-done | bytes 262168
  5.0 0.0 copy-start.3
  5.0 0.9 %copy-done.3 = bf16[1,16,4096]{2,1,0:T(8,128)(2,1)S(1)} copy-done((bf16[1,16,4096]{2,1,0:T(8,128)(2,1)S(1)}, bf16[1,16,4096]{2,1,0:T(8,128)(2,1)}, u32[]{:S(2)}) %copy-start.3) | copy-done | bytes 131096
  5.9 0.0 copy-start.4
  5.9 0.7 copy-done.4
  6.5 0.0 copy-start.5
  6.5 0.7 copy-done.5
  7.2 75.7 %shard_map.73 = bf16[512,256]{1,0:T(8,128)(2,1)S(1)} custom-call(s32[32,16]{1,0:T(8,128)S(1)} %copy.8.gsa, s32[512]{0:T(512)S(1)} %copy-done.4, s32[1,512]{1,0:T(1,128)S(1)} %bitcast.1, bf16[512,512]{1,0:T(8,128)(2,1)S(1)} %copy-done.1, bf16[8192,256]{1,0:T(8,128)(2,1)S(1)} %copy-done, bf16[1,16,8192]{2,1,0:T(8,128)(2,1)S(1)} %copy-done.2, ...), custom_call_target="tpu_custom_call" | custom-call | flops 2147483648 | bytes 8388608 | tf_op jit(solution)/shard_map/pallas_call | solution.py:311
  82.9 0.7 copy.10
Async XLA Ops:
  0.8 2.2 %copy-start = (bf16[8192,256]{1,0:T(8,128)(2,1)S(1)}, bf16[8192,256]{1,0:T(8,128)(2,1)}, u32[]{:S(2)}) copy-start(bf16[8192,256]{1,0:T(8,128)(2,1)} %w_hbm.1) | copy-start | bytes 12582916
  3.0 1.0 %copy-start.1 = (bf16[512,512]{1,0:T(8,128)(2,1)S(1)}, bf16[512,512]{1,0:T(8,128)(2,1)}, u32[]{:S(2)}) copy-start(bf16[512,512]{1,0:T(8,128)(2,1)} %tok.1) | copy-start | bytes 1572868
  4.0 0.9 %copy-start.2 = (bf16[1,16,8192]{2,1,0:T(8,128)(2,1)S(1)}, bf16[1,16,8192]{2,1,0:T(8,128)(2,1)}, u32[]{:S(2)}) copy-start(bf16[1,16,8192]{2,1,0:T(8,128)(2,1)} %down.1) | copy-start | bytes 786436
  5.0 0.9 %copy-start.3 = (bf16[1,16,4096]{2,1,0:T(8,128)(2,1)S(1)}, bf16[1,16,4096]{2,1,0:T(8,128)(2,1)}, u32[]{:S(2)}) copy-start(bf16[1,16,4096]{2,1,0:T(8,128)(2,1)} %up.1) | copy-start | bytes 393220
  5.9 0.7 copy-start.4
  6.5 0.7 copy-start.5

commit v2 on v1

v2 whole, which is shorter than its diff:
```python
import functools

import jax
import jax.numpy as jnp
from jax import lax
from jax.experimental import pallas as pl
from jax.experimental.pallas import tpu as pltpu
from jax.sharding import PartitionSpec as P

RANK = 16
SLOTS = 16
SCALE = 0.5
NZ, NX, NY, NC = 8, 4, 8, 2
NG, NT = NZ * NX, NY * NC
ROWS = 512
KB = 512
NB = 256
CH = 4
CR = ROWS // CH
VLIM = 60 * 1024
PLUS = (0, 2)
MESH = pl.DeviceIdType.MESH


def kernel(
    gsa_hbm, asp_hbm, idx_hbm, tok, w_hbm, down, up, out_ref,
    gsa, asp, idx_ref, xall, w_v, down_panel, up_panel, down_staged, up_staged, down_inbox, up_inbox, down_slots, up_slots, acc, part, rs, lr, lr2, local_of, here, opened,
    w_sem, x_sem, own_sem, table_sem,
    ya_send, ya_recv, ga_send, ga_recv,
    ring_send, ring_recv, cross_send, cross_recv,
    rs_send, rs_recv, lr_send, lr_recv,
):
    g = lax.axis_index("group")
    t = lax.axis_index("tensor")
    y = t // NC
    c = t % NC
    other = y * NC + (1 - c)

    def tensor_peer(i):
        return lax.rem(t + i, NT)

    def group_peer(j):
        return lax.rem(g + j, NG)

    barrier = pltpu.get_barrier_semaphore()

    @pl.loop(1, NT)
    def _(i):
        dst = tensor_peer(i)

        @pl.when(dst != 0)
        def _():
            pl.semaphore_signal(barrier, inc=1, device_id={"group": g, "tensor": dst}, device_id_type=MESH)

    w_copy = pltpu.make_async_copy(w_hbm, w_v, w_sem)
    x_copy = pltpu.make_async_copy(tok, xall.at[t], x_sem)
    down_own = pltpu.make_async_copy(
        down.at[0, :, pl.ds(pl.multiple_of(t * KB, KB), KB)], down_panel.at[t], own_sem.at[0])
    up_own = pltpu.make_async_copy(
        up.at[0, :, pl.ds(pl.multiple_of(t * NB, NB), NB)], up_panel.at[t], own_sem.at[1])
    tables = [
        pltpu.make_async_copy(src, dst, table_sem.at[n])
        for n, (src, dst) in enumerate(((gsa_hbm, gsa), (asp_hbm, asp), (idx_hbm, idx_ref)))
    ]
    for copy in tables:
        copy.start()
    down_own.start()
    up_own.start()
    x_copy.start()
    w_copy.start()

    @pl.when(t != 0)
    def _():
        pl.semaphore_wait(barrier, NT - 1)

    @pl.when(t == 1)
    def _():
        pl.semaphore_signal(here, inc=1, device_id={"group": g, "tensor": t - 1}, device_id_type=MESH)

    @pl.when(t == 0)
    def _():
        pl.semaphore_wait(here, 1)

    maps = (
        (down, KB, down_panel, down_staged, down_inbox, down_slots),
        (up, NB, up_panel, up_staged, up_inbox, up_slots),
    )

    def ya_copy(i, m):
        ref, width, panel = maps[m][:3]
        dst = tensor_peer(i)
        return pltpu.make_async_remote_copy(
            ref.at[0, :, pl.ds(pl.multiple_of(dst * width, width), width)], panel.at[t],
            ya_send.at[m, i], ya_recv.at[m, i], device_id={"group": g, "tensor": dst}, device_id_type=MESH)

    def ya_start(m):
        @pl.loop(1, NT)
        def _(i):
            ya_copy(i, m).start()

    def ya_landed(i, m):
        block = maps[m][2].at[lax.rem(t + NT - i, NT)]
        return pltpu.make_async_remote_copy(
            block, block, ya_send.at[m, i], ya_recv.at[m, i],
            device_id={"group": g, "tensor": tensor_peer(i)}, device_id_type=MESH)

    def ring_copy(src, block, d, k, way):
        dst_y = lax.rem(y + (1 if way == 0 else NY - 1), NY)
        rows = slice(k * CR, (k + 1) * CR)
        return pltpu.make_async_remote_copy(
            src.at[rows, :], xall.at[block, rows, :],
            ring_send.at[way, d - 1, k], ring_recv.at[way, d - 1, k],
            device_id={"group": g, "tensor": dst_y * NC + c}, device_id_type=MESH)

    def cross_copy(src, block, h, k):
        rows = slice(k * CR, (k + 1) * CR)
        return pltpu.make_async_remote_copy(
            src.at[rows, :], xall.at[block, rows, :],
            cross_send.at[h, k], cross_recv.at[h, k],
            device_id={"group": g, "tensor": other}, device_id_type=MESH)

    def reaches(way, d, k):
        if d < NY // 2:
            return True
        return d == NY // 2 and (k in PLUS) == (way == 0)

    def source(way, d):
        ys = lax.rem(y + (NY - d if way == 0 else d), NY)
        return ys * NC + c, ys * NC + (1 - c)

    def own_sends():
        for k in range(CH):
            for way in (0, 1):
                ring_copy(tok, t, 1, k, way).start()
            cross_copy(tok, t, 0, k).start()

    def greet_groups():
        @pl.when(t == 0)
        def _():
            @pl.loop(1, NG)
            def _(j):
                pl.semaphore_signal(
                    barrier, inc=1, device_id={"group": group_peer(j), "tensor": t}, device_id_type=MESH)

    def pick_adapters():
        for copy in tables:
            copy.wait()

        @pl.loop(0, NG)
        def _(r):
            pick = jnp.int32(0)
            for s in range(SLOTS):
                place = asp[gsa[s, r]]
                pick = pick + jnp.where(lax.shift_right_logical(place, 4) == g, place & 15, 0)
            local_of[r] = pick

    def panel_wait(m):
        (down_own, up_own)[m].wait()

        @pl.loop(1, NT)
        def _(i):
            ya_landed(i, m).wait_recv()

    def groups_wait():
        @pl.when(t == 0)
        def _():
            pl.semaphore_wait(barrier, NG - 1)

            @pl.loop(1, NT)
            def _(i):
                pl.semaphore_signal(
                    opened, inc=1, device_id={"group": g, "tensor": tensor_peer(i)}, device_id_type=MESH)

        @pl.when(t != 0)
        def _():
            pl.semaphore_wait(opened, 1)

    def ga_copy(j, m):
        staged, inbox = maps[m][3:5]
        dst = group_peer(j)
        return pltpu.make_async_remote_copy(
            staged.at[j], inbox.at[g],
            ga_send.at[m, j], ga_recv.at[m, j], device_id={"group": dst, "tensor": t}, device_id_type=MESH)

    def send_adapters(m):
        panel, staged, inbox = maps[m][2:5]

        @pl.loop(1, NG)
        def _(j):
            staged[j] = panel[local_of[group_peer(j)]]
            ga_copy(j, m).start()

        inbox[g] = panel[local_of[g]]

    def adapters_wait(m):
        inbox, slots = maps[m][4:]

        @pl.loop(1, NG)
        def _(j):
            block = inbox.at[lax.rem(g + NG - j, NG)]
            pltpu.make_async_remote_copy(
                block, block, ga_send.at[m, j], ga_recv.at[m, j],
                device_id={"group": group_peer(j), "tensor": t}, device_id_type=MESH).wait_recv()

        for s in range(SLOTS):
            owner = lax.shift_right_logical(asp[gsa[s, g]], 4)
            slots[s * RANK:(s + 1) * RANK, :] = inbox[owner]

    def weight(block):
        return w_v[pl.ds(pl.multiple_of(block * KB, KB), KB), :]

    def accumulate(block, first=False):
        term = jnp.dot(xall[block], weight(block), preferred_element_type=jnp.float32)
        if first:
            acc[...] = term
        else:
            acc[...] += term

    def ring_step(d, ks=range(CH)):
        for k in ks:
            for way in (0, 1):
                if not reaches(way, d, k):
                    continue
                block, _ = source(way, d)
                ring_copy(xall.at[block], block, d, k, way).wait_recv()
                if reaches(way, d + 1, k):
                    ring_copy(xall.at[block], block, d + 1, k, way).start()
                h = d if way == 0 or d == NY // 2 else NY - d
                cross_copy(xall.at[block], block, h, k).start()

    def blocks_at(d):
        return (0,) if d == NY // 2 else (0, 1)

    def ring_own(d):
        if d == 0:
            accumulate(t, True)
            return
        for way in blocks_at(d):
            accumulate(source(way, d)[0])

    def ring_cross(d):
        for way in blocks_at(d) if d else (0,):
            h = d if way == 0 else NY - d
            block = source(way, d)[1]
            for k in range(CH):
                cross_copy(xall.at[block], block, h, k).wait_recv()
            accumulate(block)

    def rs_copy(i):
        dst = tensor_peer(i)
        return pltpu.make_async_remote_copy(
            part.at[dst], rs.at[t], rs_send.at[i], rs_recv.at[i],
            device_id={"group": g, "tensor": dst}, device_id_type=MESH)

    def lr_copy(i):
        return pltpu.make_async_remote_copy(
            lr.at[t], lr.at[t], lr_send.at[i], lr_recv.at[i],
            device_id={"group": g, "tensor": tensor_peer(i)}, device_id_type=MESH)

    def shrink():
        adapters_wait(0)
        idx = idx_ref[...]
        every = lax.dot_general(
            down_slots[...], xall[t], (((1,), (1,)), ((), ())), preferred_element_type=jnp.float32)
        partial = jnp.zeros((RANK, ROWS), jnp.float32)
        for s in range(SLOTS):
            partial = partial + jnp.where(idx == s, every[s * RANK:(s + 1) * RANK, :], 0.0)
        for r in range(RANK):
            part[r] = partial[r:r + 1, :]

        @pl.loop(1, NT)
        def _(i):
            rs_copy(i).start()

        rs[t] = part[t]

    def sum_shrink():
        @pl.loop(1, NT)
        def _(i):
            src = lax.rem(t + NT - i, NT)
            pltpu.make_async_remote_copy(
                rs.at[src], rs.at[src], rs_send.at[i], rs_recv.at[i],
                device_id={"group": g, "tensor": tensor_peer(i)}, device_id_type=MESH).wait_recv()

        total = rs[0]
        for i in range(1, NT):
            total = total + rs[i]
        lr[t] = total

        @pl.loop(1, NT)
        def _(i):
            lr_copy(i).start()

    def early_sends():
        @pl.loop(1, NT)
        def _(i):
            ya_copy(i, 0).wait_send()
            ya_copy(i, 1).wait_send()
            rs_copy(i).wait_send()

        @pl.loop(1, NG)
        def _(j):
            ga_copy(j, 0).wait_send()
            ga_copy(j, 1).wait_send()

    def ring_sent(d):
        for k in range(CH):
            for way in (0, 1):
                if reaches(way, d, k):
                    ring_copy(xall.at[t], t, d, k, way).wait_send()

    def cross_sent(h):
        for k in range(CH):
            cross_copy(xall.at[t], t, h, k).wait_send()

    def lr_sent():
        @pl.loop(1, NT)
        def _(i):
            lr_copy(i).wait_send()

    def expand():
        @pl.loop(1, NT)
        def _(i):
            src = lax.rem(t + NT - i, NT)
            pltpu.make_async_remote_copy(
                lr.at[src], lr.at[src], lr_send.at[i], lr_recv.at[i],
                device_id={"group": g, "tensor": tensor_peer(i)}, device_id_type=MESH).wait_recv()

        for r in range(RANK):
            lr2[r:r + 1, :] = lr[r]
        low = lr2[...].astype(jnp.bfloat16).astype(jnp.float32)
        idx = idx_ref[...]
        spread = jnp.concatenate([jnp.where(idx == s, low, 0.0) for s in range(SLOTS)], axis=0)
        spread = jnp.transpose(spread).astype(jnp.bfloat16)
        adapter = jnp.dot(spread, up_slots[...], preferred_element_type=jnp.float32)
        acc[...] += SCALE * adapter

    def operands_wait():
        x_copy.wait()
        w_copy.wait()

    ya_start(0)
    own_sends()
    ya_start(1)
    greet_groups()
    pick_adapters()
    operands_wait()
    panel_wait(0)
    groups_wait()
    send_adapters(0)
    ring_own(0)
    ring_step(1)
    panel_wait(1)
    send_adapters(1)
    ring_step(2, range(CH // 2))
    shrink()
    ring_step(2, range(CH // 2, CH))
    ring_own(1)
    ring_cross(0)
    ring_step(3, range(CH // 2))
    sum_shrink()
    ring_step(3, range(CH // 2, CH))
    ring_own(2)
    ring_cross(1)
    early_sends()
    ring_cross(2)
    ring_own(3)
    ring_sent(1)
    ring_sent(2)
    ring_sent(3)
    for h in (0, 1, 2, 6, 7):
        cross_sent(h)
    adapters_wait(1)
    ring_step(4)
    ring_cross(3)
    cross_sent(3)
    cross_sent(5)
    expand()
    lr_sent()
    ring_own(4)
    ring_cross(4)

    out_ref[...] = acc[...].astype(out_ref.dtype)
    ring_sent(NY // 2)
    cross_sent(NY // 2)


def body(tokens, token_slot_index, group_slot_adapters, adapter_storage_position, query_weight, down_weight, up_weight):
    hbm = pl.BlockSpec(memory_space=pltpu.HBM)
    vmem = pl.BlockSpec(memory_space=pltpu.VMEM)
    dma = pltpu.SemaphoreType.DMA
    bf16, f32 = jnp.bfloat16, jnp.float32
    return pl.pallas_call(
        kernel,
        out_shape=jax.ShapeDtypeStruct((ROWS, NB), bf16),
        in_specs=[hbm] * 7,
        out_specs=vmem,
        scratch_shapes=[
            pltpu.SMEM((SLOTS, NG), jnp.int32),
            pltpu.SMEM((NT * NG,), jnp.int32),
            pltpu.VMEM((1, ROWS), jnp.int32),
            pltpu.VMEM((NT, ROWS, KB), bf16),
            pltpu.VMEM((NT * KB, NB), bf16),
            pltpu.VMEM((NT, RANK, KB), bf16),
            pltpu.VMEM((NT, RANK, NB), bf16),
            pltpu.VMEM((NG, RANK, KB), bf16),
            pltpu.VMEM((NG, RANK, NB), bf16),
            pltpu.VMEM((NG, RANK, KB), bf16),
            pltpu.VMEM((NG, RANK, NB), bf16),
            pltpu.VMEM((SLOTS * RANK, KB), bf16),
            pltpu.VMEM((SLOTS * RANK, NB), bf16),
            pltpu.VMEM((ROWS, NB), f32),
            pltpu.VMEM((RANK, 1, ROWS), f32),
            pltpu.VMEM((NT, 1, ROWS), f32),
            pltpu.VMEM((NT, 1, ROWS), f32),
            pltpu.VMEM((RANK, ROWS), f32),
            pltpu.SMEM((NG,), jnp.int32),
            pltpu.SemaphoreType.REGULAR, pltpu.SemaphoreType.REGULAR,
            dma, dma, dma((2,)), dma((3,)),
            dma((2, NT)), dma((2, NT)), dma((2, NG)), dma((2, NG)),
            dma((2, NY // 2, CH)), dma((2, NY // 2, CH)), dma((NY, CH)), dma((NY, CH)),
            dma((NT,)), dma((NT,)), dma((NT,)), dma((NT,)),
        ],
        compiler_params=pltpu.CompilerParams(
            collective_id=0, has_side_effects=True, vmem_limit_bytes=VLIM * 1024),
        cost_estimate=pl.CostEstimate(flops=2 * ROWS * NT * KB * NB, bytes_accessed=8 << 20, transcendentals=0),
    )(group_slot_adapters.T, adapter_storage_position, token_slot_index.reshape(1, ROWS),
      tokens, query_weight, down_weight, up_weight)


def solution(mesh):
    in_specs = (
        P("group", "tensor"),
        P("group"),
        P(),
        P(),
        P(None, "tensor"),
        P(("group", "tensor"), None, None),
        P(("group", "tensor"), None, None),
    )
    return jax.shard_map(body, mesh=mesh, in_specs=in_specs, out_specs=P("group", "tensor"), check_vma=False)
```

time: 84 us -> 68.9 us (0.82)
  Pallas kernels: 75.7 us -> 67 us
  local copies, waits for them, and re-layouts: 7.92 us -> 1.67 us
    pallas_call x1, Pallas kernels: 75.7 us -> 67 us  [body(): pl.pallas_call(kernel, out_shape=jax.ShapeDtypeStruct((ROWS, NB), bf16),...]
    unnamed x14 -> x1, local copies, waits for them, and re-layouts: 7.92 us -> 1.67 us
where the time goes in v2:
time: 68.9 us; the launch traced here: 68.7 us
  Pallas kernels  67 us (97%)
  local copies, waits for them, and re-layouts  1.67 us (2%)
    pallas_call x1, Pallas kernels, body(): pl.pallas_call(kernel, out_shape=jax.ShapeDtypeStruct((ROWS, NB), bf16),...  67 us
    unnamed x1, local copies, waits for them, and re-layouts  1.67 us

profile of v2, /device:TPU:1, one launch (start us, length us, event | category | flops | bytes accessed | tf_op | source)
XLA Modules:
  0.0 68.7 jit_solution(14717718715935283176)
XLA Ops:
  0.0 67.0 %shard_map.73 = bf16[512,256]{1,0:T(8,128)(2,1)} custom-call(s32[16,32]{1,0:T(8,128)} %bitcast.2, s32[512]{0:T(512)} %asp_hbm.1, s32[1,512]{1,0:T(1,128)} %bitcast.3, bf16[512,512]{1,0:T(8,128)(2,1)} %tok.1, bf16[8192,256]{1,0:T(8,128)(2,1)} %w_hbm.1, bf16[1,16,8192]{2,1,0:T(8,128)(2,1)} %down.1, bf16[1,16,4096]{2,1,0:T(8,128)(2,1)} %up.1), custom_call_target="tpu_custom_call" | custom-call | flops 2147483648 | bytes 8388608 | tf_op jit(solution)/shard_map/pallas_call | solution.py:393
  67.1 1.7 %copy.9 = bf16[512,256]{1,0:T(8,128)(2,1)} copy(bf16[512,256]{1,0:T(8,128)(2,1)} %shard_map.73) | data formatting | bytes 524288

commit v3 on v2

--- a/solution.py
+++ b/solution.py
@@ -17,7 +17,7 @@
 NB = 256
 CH = 4
 CR = ROWS // CH
-VLIM = 60 * 1024
+VLIM = 40 * 1024
 PLUS = (0, 2)
 MESH = pl.DeviceIdType.MESH
 
@@ -81,6 +81,10 @@
     def _():
         pl.semaphore_wait(here, 1)
 
+    def settled(block, send_sem, recv_sem):
+        return pltpu.make_async_remote_copy(
+            block, block, send_sem, recv_sem, device_id={"group": g, "tensor": other}, device_id_type=MESH)
+
     maps = (
         (down, KB, down_panel, down_staged, down_inbox, down_slots),
         (up, NB, up_panel, up_staged, up_inbox, up_slots),
@@ -91,33 +95,36 @@
         dst = tensor_peer(i)
         return pltpu.make_async_remote_copy(
             ref.at[0, :, pl.ds(pl.multiple_of(dst * width, width), width)], panel.at[t],
-            ya_send.at[m, i], ya_recv.at[m, i], device_id={"group": g, "tensor": dst}, device_id_type=MESH)
+            ya_send.at[m], ya_recv.at[m], device_id={"group": g, "tensor": dst}, device_id_type=MESH)
 
     def ya_start(m):
         @pl.loop(1, NT)
         def _(i):
             ya_copy(i, m).start()
 
-    def ya_landed(i, m):
-        block = maps[m][2].at[lax.rem(t + NT - i, NT)]
-        return pltpu.make_async_remote_copy(
-            block, block, ya_send.at[m, i], ya_recv.at[m, i],
-            device_id={"group": g, "tensor": tensor_peer(i)}, device_id_type=MESH)
+    def ya_all(m):
+        return settled(maps[m][2].at[pl.ds(0, NT - 1)], ya_send.at[m], ya_recv.at[m])
 
     def ring_copy(src, block, d, k, way):
         dst_y = lax.rem(y + (1 if way == 0 else NY - 1), NY)
         rows = slice(k * CR, (k + 1) * CR)
-        return pltpu.make_async_remote_copy(
-            src.at[rows, :], xall.at[block, rows, :],
-            ring_send.at[way, d - 1, k], ring_recv.at[way, d - 1, k],
+        n = (d - 1) * 2 * CH + (2 * k + way if d < NY // 2 else k)
+        return pltpu.make_async_remote_copy(
+            src.at[rows, :], xall.at[block, rows, :], ring_send, ring_recv.at[n],
             device_id={"group": g, "tensor": dst_y * NC + c}, device_id_type=MESH)
 
     def cross_copy(src, block, h, k):
         rows = slice(k * CR, (k + 1) * CR)
-        return pltpu.make_async_remote_copy(
-            src.at[rows, :], xall.at[block, rows, :],
-            cross_send.at[h, k], cross_recv.at[h, k],
+        n = NY if h == NY // 2 and k >= CH // 2 else h
+        return pltpu.make_async_remote_copy(
+            src.at[rows, :], xall.at[block, rows, :], cross_send, cross_recv.at[n],
             device_id={"group": g, "tensor": other}, device_id_type=MESH)
+
+    def cross_all(h):
+        block = xall.at[0]
+        if h in (NY // 2, NY):
+            block = xall.at[0, pl.ds(0, ROWS // 2)]
+        return settled(block, cross_send, cross_recv.at[h])
 
     def reaches(way, d, k):
         if d < NY // 2:
@@ -157,9 +164,7 @@
     def panel_wait(m):
         (down_own, up_own)[m].wait()
 
-        @pl.loop(1, NT)
-        def _(i):
-            ya_landed(i, m).wait_recv()
+        ya_all(m).wait_recv()
 
     def groups_wait():
         @pl.when(t == 0)
@@ -180,7 +185,7 @@
         dst = group_peer(j)
         return pltpu.make_async_remote_copy(
             staged.at[j], inbox.at[g],
-            ga_send.at[m, j], ga_recv.at[m, j], device_id={"group": dst, "tensor": t}, device_id_type=MESH)
+            ga_send.at[m], ga_recv.at[m], device_id={"group": dst, "tensor": t}, device_id_type=MESH)
 
     def send_adapters(m):
         panel, staged, inbox = maps[m][2:5]
@@ -192,15 +197,13 @@
 
         inbox[g] = panel[local_of[g]]
 
+    def ga_all(m):
+        return settled(maps[m][4].at[pl.ds(0, NG - 1)], ga_send.at[m], ga_recv.at[m])
+
     def adapters_wait(m):
         inbox, slots = maps[m][4:]
 
-        @pl.loop(1, NG)
-        def _(j):
-            block = inbox.at[lax.rem(g + NG - j, NG)]
-            pltpu.make_async_remote_copy(
-                block, block, ga_send.at[m, j], ga_recv.at[m, j],
-                device_id={"group": group_peer(j), "tensor": t}, device_id_type=MESH).wait_recv()
+        ga_all(m).wait_recv()
 
         for s in range(SLOTS):
             owner = lax.shift_right_logical(asp[gsa[s, g]], 4)
@@ -215,6 +218,15 @@
             acc[...] = term
         else:
             acc[...] += term
+
+    def close(part_rows):
+        far, far_other = source(0, NY // 2)
+        rows = pl.ds(part_rows * (ROWS // 2), ROWS // 2)
+        value = acc[rows, :] + jnp.dot(xall[far, rows, :], weight(far), preferred_element_type=jnp.float32)
+        cross_all(NY if part_rows else NY // 2).wait_recv()
+        value = value + jnp.dot(
+            xall[far_other, rows, :], weight(far_other), preferred_element_type=jnp.float32)
+        out_ref[rows, :] = value.astype(out_ref.dtype)
 
     def ring_step(d, ks=range(CH)):
         for k in ks:
@@ -242,19 +254,24 @@
         for way in blocks_at(d) if d else (0,):
             h = d if way == 0 else NY - d
             block = source(way, d)[1]
-            for k in range(CH):
-                cross_copy(xall.at[block], block, h, k).wait_recv()
+            cross_all(h).wait_recv()
             accumulate(block)
 
     def rs_copy(i):
         dst = tensor_peer(i)
         return pltpu.make_async_remote_copy(
-            part.at[dst], rs.at[t], rs_send.at[i], rs_recv.at[i],
+            part.at[dst], rs.at[t], rs_send, rs_recv,
             device_id={"group": g, "tensor": dst}, device_id_type=MESH)
 
+    def rs_all():
+        return settled(rs.at[pl.ds(0, NT - 1)], rs_send, rs_recv)
+
+    def lr_all():
+        return settled(lr.at[pl.ds(0, NT - 1)], lr_send, lr_recv)
+
     def lr_copy(i):
         return pltpu.make_async_remote_copy(
-            lr.at[t], lr.at[t], lr_send.at[i], lr_recv.at[i],
+            lr.at[t], lr.at[t], lr_send, lr_recv,
             device_id={"group": g, "tensor": tensor_peer(i)}, device_id_type=MESH)
 
     def shrink():
@@ -275,12 +292,7 @@
         rs[t] = part[t]
 
     def sum_shrink():
-        @pl.loop(1, NT)
-        def _(i):
-            src = lax.rem(t + NT - i, NT)
-            pltpu.make_async_remote_copy(
-                rs.at[src], rs.at[src], rs_send.at[i], rs_recv.at[i],
-                device_id={"group": g, "tensor": tensor_peer(i)}, device_id_type=MESH).wait_recv()
+        rs_all().wait_recv()
 
         total = rs[0]
         for i in range(1, NT):
@@ -292,39 +304,18 @@
             lr_copy(i).start()
 
     def early_sends():
-        @pl.loop(1, NT)
-        def _(i):
-            ya_copy(i, 0).wait_send()
-            ya_copy(i, 1).wait_send()
-            rs_copy(i).wait_send()
-
-        @pl.loop(1, NG)
-        def _(j):
-            ga_copy(j, 0).wait_send()
-            ga_copy(j, 1).wait_send()
-
-    def ring_sent(d):
-        for k in range(CH):
-            for way in (0, 1):
-                if reaches(way, d, k):
-                    ring_copy(xall.at[t], t, d, k, way).wait_send()
-
-    def cross_sent(h):
-        for k in range(CH):
-            cross_copy(xall.at[t], t, h, k).wait_send()
-
-    def lr_sent():
-        @pl.loop(1, NT)
-        def _(i):
-            lr_copy(i).wait_send()
+        for m in (0, 1):
+            ya_all(m).wait_send()
+            ga_all(m).wait_send()
+        rs_all().wait_send()
+
+    def last_sends():
+        lr_all().wait_send()
+        settled(xall.at[pl.ds(0, NY - 1)], ring_send, ring_recv.at[0]).wait_send()
+        settled(xall.at[pl.ds(0, NY)], cross_send, cross_recv.at[0]).wait_send()
 
     def expand():
-        @pl.loop(1, NT)
-        def _(i):
-            src = lax.rem(t + NT - i, NT)
-            pltpu.make_async_remote_copy(
-                lr.at[src], lr.at[src], lr_send.at[i], lr_recv.at[i],
-                device_id={"group": g, "tensor": tensor_peer(i)}, device_id_type=MESH).wait_recv()
+        lr_all().wait_recv()
 
         for r in range(RANK):
             lr2[r:r + 1, :] = lr[r]
@@ -365,24 +356,15 @@
     early_sends()
     ring_cross(2)
     ring_own(3)
-    ring_sent(1)
-    ring_sent(2)
-    ring_sent(3)
-    for h in (0, 1, 2, 6, 7):
-        cross_sent(h)
     adapters_wait(1)
-    ring_step(4)
+    ring_step(4, range(CH // 2))
     ring_cross(3)
-    cross_sent(3)
-    cross_sent(5)
     expand()
-    lr_sent()
-    ring_own(4)
-    ring_cross(4)
-
-    out_ref[...] = acc[...].astype(out_ref.dtype)
-    ring_sent(NY // 2)
-    cross_sent(NY // 2)
+    close(0)
+    ring_step(4, range(CH // 2, CH))
+    close(1)
+
+    last_sends()
 
 
 def body(tokens, token_slot_index, group_slot_adapters, adapter_storage_position, query_weight, down_weight, up_weight):
@@ -417,15 +399,16 @@
             pltpu.SMEM((NG,), jnp.int32),
             pltpu.SemaphoreType.REGULAR, pltpu.SemaphoreType.REGULAR,
             dma, dma, dma((2,)), dma((3,)),
-            dma((2, NT)), dma((2, NT)), dma((2, NG)), dma((2, NG)),
-            dma((2, NY // 2, CH)), dma((2, NY // 2, CH)), dma((NY, CH)), dma((NY, CH)),
-            dma((NT,)), dma((NT,)), dma((NT,)), dma((NT,)),
+            dma((2,)), dma((2,)), dma((2,)), dma((2,)),
+            dma, dma(((NY - 1) * CH,)), dma, dma((NY + 1,)),
+            dma, dma, dma, dma,
         ],
         compiler_params=pltpu.CompilerParams(
             collective_id=0, has_side_effects=True, vmem_limit_bytes=VLIM * 1024),
         cost_estimate=pl.CostEstimate(flops=2 * ROWS * NT * KB * NB, bytes_accessed=8 << 20, transcendentals=0),
-    )(group_slot_adapters.T, adapter_storage_position, token_slot_index.reshape(1, ROWS),
-      tokens, query_weight, down_weight, up_weight)
+    )(*(pltpu.with_memory_space_constraint(x, pltpu.HBM) for x in (
+        group_slot_adapters.T, adapter_storage_position, token_slot_index.reshape(1, ROWS),
+        tokens, query_weight, down_weight, up_weight)))
 
 
 def solution(mesh):

time: 68.9 us -> 64.9 us (0.942)
  Pallas kernels: 67 us -> 64.1 us
  local copies, waits for them, and re-layouts: 1.67 us -> 0.71 us
    pallas_call x1, Pallas kernels: 67 us -> 64.1 us  [body(): pl.pallas_call(kernel, out_shape=jax.ShapeDtypeStruct((ROWS, NB), bf16),...]
    unnamed x1, local copies, waits for them, and re-layouts: 1.67 us -> 0.71 us
where the time goes in v3:
time: 64.9 us; the launch traced here: 64.8 us
  Pallas kernels  64.1 us (99%)
  local copies, waits for them, and re-layouts  0.71 us (1%)
    pallas_call x1, Pallas kernels, body(): pl.pallas_call(kernel, out_shape=jax.ShapeDtypeStruct((ROWS, NB), bf16),...  64.1 us

profile of v3, /device:TPU:1, one launch (start us, length us, event | category | flops | bytes accessed | tf_op | source)
XLA Modules:
  0.0 64.8 jit_solution(2951501509281378005)
XLA Ops:
  0.0 64.1 %shard_map.73 = bf16[512,256]{1,0:T(8,128)(2,1)S(1)} custom-call(s32[16,32]{1,0:T(8,128)} %bitcast.2, s32[512]{0:T(512)} %asp_hbm.1, s32[1,512]{1,0:T(1,128)} %bitcast.3, bf16[512,512]{1,0:T(8,128)(2,1)} %tok.1, bf16[8192,256]{1,0:T(8,128)(2,1)} %w_hbm.1, bf16[1,16,8192]{2,1,0:T(8,128)(2,1)} %down.1, bf16[1,16,4096]{2,1,0:T(8,128)(2,1)} %up.1), custom_call_target="tpu_custom_call" | custom-call | flops 2147483648 | bytes 8388608 | tf_op jit(solution)/shard_map/pallas_call | solution.py:375
  64.1 0.7 %copy.9 = bf16[512,256]{1,0:T(8,128)(2,1)} copy(bf16[512,256]{1,0:T(8,128)(2,1)S(1)} %shard_map.73) | data formatting | bytes 524288

commit v4 on v3

--- a/solution.py
+++ b/solution.py
@@ -37,10 +37,10 @@
     other = y * NC + (1 - c)
 
     def tensor_peer(i):
-        return lax.rem(t + i, NT)
+        return lax.rem(t + NT + (2 * lax.rem(i, 2) - 1) * lax.div(i + 1, 2), NT)
 
     def group_peer(j):
-        return lax.rem(g + j, NG)
+        return lax.rem(g + NG + (2 * lax.rem(j, 2) - 1) * lax.div(j + 1, 2), NG)
 
     barrier = pltpu.get_barrier_semaphore()
 
@@ -343,14 +343,12 @@
     ring_step(1)
     panel_wait(1)
     send_adapters(1)
-    ring_step(2, range(CH // 2))
     shrink()
-    ring_step(2, range(CH // 2, CH))
+    ring_step(2)
     ring_own(1)
     ring_cross(0)
-    ring_step(3, range(CH // 2))
     sum_shrink()
-    ring_step(3, range(CH // 2, CH))
+    ring_step(3)
     ring_own(2)
     ring_cross(1)
     early_sends()
@@ -363,7 +361,6 @@
     close(0)
     ring_step(4, range(CH // 2, CH))
     close(1)
-
     last_sends()
 
 

time: 64.9 us -> 63.9 us (0.985)
  Pallas kernels: 64.1 us -> 63 us
    pallas_call x1, Pallas kernels: 64.1 us -> 63 us  [body(): pl.pallas_call(kernel, out_shape=jax.ShapeDtypeStruct((ROWS, NB), bf16),...]
where the time goes in v4:
time: 63.9 us; the launch traced here: 63.7 us
  Pallas kernels  63 us (99%)
  local copies, waits for them, and re-layouts  0.71 us (1%)
    pallas_call x1, Pallas kernels, body(): pl.pallas_call(kernel, out_shape=jax.ShapeDtypeStruct((ROWS, NB), bf16),...  63 us

profile of v4, /device:TPU:1, one launch (start us, length us, event | category | flops | bytes accessed | tf_op | source)
XLA Modules:
  0.0 63.7 jit_solution(442812564093373740)
XLA Ops:
  0.0 63.0 %shard_map.73 = bf16[512,256]{1,0:T(8,128)(2,1)S(1)} custom-call(s32[16,32]{1,0:T(8,128)} %bitcast.2, s32[512]{0:T(512)} %asp_hbm.1, s32[1,512]{1,0:T(1,128)} %bitcast.3, bf16[512,512]{1,0:T(8,128)(2,1)} %tok.1, bf16[8192,256]{1,0:T(8,128)(2,1)} %w_hbm.1, bf16[1,16,8192]{2,1,0:T(8,128)(2,1)} %down.1, bf16[1,16,4096]{2,1,0:T(8,128)(2,1)} %up.1), custom_call_target="tpu_custom_call" | custom-call | flops 2147483648 | bytes 8388608 | tf_op jit(solution)/shard_map/pallas_call | solution.py:372
  63.0 0.7 %copy.9 = bf16[512,256]{1,0:T(8,128)(2,1)} copy(bf16[512,256]{1,0:T(8,128)(2,1)S(1)} %shard_map.73) | data formatting | bytes 524288

commit v5 on v4

--- a/solution.py
+++ b/solution.py
@@ -354,12 +354,12 @@
     early_sends()
     ring_cross(2)
     ring_own(3)
-    adapters_wait(1)
     ring_step(4, range(CH // 2))
     ring_cross(3)
+    ring_step(4, range(CH // 2, CH))
+    adapters_wait(1)
     expand()
     close(0)
-    ring_step(4, range(CH // 2, CH))
     close(1)
     last_sends()
 

time: 63.9 us -> 63.9 us (level)
  no operation moved by 1% of the time
where the time goes in v5:
time: 63.9 us; the launch traced here: 63.7 us
  Pallas kernels  63 us (99%)
  local copies, waits for them, and re-layouts  0.71 us (1%)
    pallas_call x1, Pallas kernels, body(): pl.pallas_call(kernel, out_shape=jax.ShapeDtypeStruct((ROWS, NB), bf16),...  63 us

profile of v5, /device:TPU:1, one launch (start us, length us, event | category | flops | bytes accessed | tf_op | source)
XLA Modules:
  0.0 63.7 jit_solution(17998252579482425528)
XLA Ops:
  0.0 63.0 %shard_map.73 = bf16[512,256]{1,0:T(8,128)(2,1)S(1)} custom-call(s32[16,32]{1,0:T(8,128)} %bitcast.2, s32[512]{0:T(512)} %asp_hbm.1, s32[1,512]{1,0:T(1,128)} %bitcast.3, bf16[512,512]{1,0:T(8,128)(2,1)} %tok.1, bf16[8192,256]{1,0:T(8,128)(2,1)} %w_hbm.1, bf16[1,16,8192]{2,1,0:T(8,128)(2,1)} %down.1, bf16[1,16,4096]{2,1,0:T(8,128)(2,1)} %up.1), custom_call_target="tpu_custom_call" | custom-call | flops 2147483648 | bytes 8388608 | tf_op jit(solution)/shard_map/pallas_call | solution.py:372
  63.0 0.7 %copy.9 = bf16[512,256]{1,0:T(8,128)(2,1)} copy(bf16[512,256]{1,0:T(8,128)(2,1)S(1)} %shard_map.73) | data formatting | bytes 524288

commit v6 on v5

--- a/solution.py
+++ b/solution.py
@@ -66,8 +66,6 @@
         copy.start()
     down_own.start()
     up_own.start()
-    x_copy.start()
-    w_copy.start()
 
     @pl.when(t != 0)
     def _():
@@ -333,6 +331,8 @@
     ya_start(0)
     own_sends()
     ya_start(1)
+    x_copy.start()
+    w_copy.start()
     greet_groups()
     pick_adapters()
     operands_wait()

time: 63.9 us -> 63.9 us (level)
  no operation moved by 1% of the time
where the time goes in v6:
time: 63.9 us; the launch traced here: 63.7 us
  Pallas kernels  63 us (99%)
  local copies, waits for them, and re-layouts  0.71 us (1%)
    pallas_call x1, Pallas kernels, body(): pl.pallas_call(kernel, out_shape=jax.ShapeDtypeStruct((ROWS, NB), bf16),...  63 us

profile of v6, /device:TPU:1, one launch (start us, length us, event | category | flops | bytes accessed | tf_op | source)
XLA Modules:
  0.0 63.7 jit_solution(17970387078873359022)
XLA Ops:
  0.0 63.0 %shard_map.73 = bf16[512,256]{1,0:T(8,128)(2,1)S(1)} custom-call(s32[16,32]{1,0:T(8,128)} %bitcast.2, s32[512]{0:T(512)} %asp_hbm.1, s32[1,512]{1,0:T(1,128)} %bitcast.3, bf16[512,512]{1,0:T(8,128)(2,1)} %tok.1, bf16[8192,256]{1,0:T(8,128)(2,1)} %w_hbm.1, bf16[1,16,8192]{2,1,0:T(8,128)(2,1)} %down.1, bf16[1,16,4096]{2,1,0:T(8,128)(2,1)} %up.1), custom_call_target="tpu_custom_call" | custom-call | flops 2147483648 | bytes 8388608 | tf_op jit(solution)/shard_map/pallas_call | solution.py:372
  63.0 0.7 %copy.9 = bf16[512,256]{1,0:T(8,128)(2,1)} copy(bf16[512,256]{1,0:T(8,128)(2,1)S(1)} %shard_map.73) | data formatting | bytes 524288
